TPU v7x, 32 devices: a whole 2x2x4 slice. The times are simulated.
32 devices in a mesh: side: 2 (over core), grp: 4 (over y, x), ex: 4 (over z).
Axes of the slice: x: 2, y: 2, z: 4, core: 2. Of those that a mesh axis runs over, the one named last changes fastest.
Arguments:
- tokens: bfloat16 [48, 7168], P(('grp', 'ex'), 'side'), may hold values from -6 to 6
- expert_ids: int32 [48, 8], P(('grp', 'ex')), may hold values from 0 to 15, all different within a row; in each aligned block of 3 rows (0 to 2, 3 to 5, ...) at most 3 rows name the same one
- scores: float32 [48, 8], P(('grp', 'ex')), may hold values from -8 to 8
- gate_weight: bfloat16 [16, 7168, 2048], P('ex', 'side', 'grp'), may hold values from -0.0625 to 0.0625
- up_weight: bfloat16 [16, 7168, 2048], P('ex', 'side', 'grp'), may hold values from -0.0625 to 0.0625
- down_weight: bfloat16 [16, 2048, 7168], P('ex', None, ('side', 'grp')), may hold values from -0.125 to 0.125
Outputs:
- combined: bfloat16 [48, 7168], P(('grp', 'ex'), 'side')
Inputs may be any that keep to these rules, and one draw needn't show every extreme that they name: `expert_ids`: each row names 8 different experts; every expert is named by some row.
All inputs are finite; a program needn't handle non-finite values.
Results may differ from a plain program's by a relative error of at most 0.011.
Values may be sent and summed in bfloat16 or wider, within the bound.
A program may use at most 192 MiB of HBM per device.

v0:
```python
import jax
import jax.numpy as jnp
from jax import lax
from jax.sharding import PartitionSpec as P


def make_fold(table, piece):
    return jnp.einsum("sech,ehd->secd", piece, table, preferred_element_type=jnp.float32)


def per_device(tokens, expert_ids, scores, gate_weight, up_weight, down_weight):
    side_count = lax.axis_size("side")
    group_count = lax.axis_size("grp")
    owner_count = lax.axis_size("ex")
    local_experts = gate_weight.shape[0]
    expert_total = local_experts * owner_count
    capacity = tokens.shape[0]
    token_count = tokens.shape[0]
    top_count = expert_ids.shape[1]
    half_width = tokens.shape[1]
    local_hidden = gate_weight.shape[2]
    share_hidden = local_hidden // side_count
    rows_total = group_count * owner_count
    flat_ids = expert_ids.reshape(-1)
    onehot = (flat_ids[:, None] == jnp.arange(expert_total, dtype=jnp.int32)[None, :]).astype(
        jnp.int32
    )
    earlier = jnp.cumsum(onehot, axis=0) - onehot
    slot_of = jnp.sum(earlier * onehot, axis=1)
    target = flat_ids * capacity + slot_of
    placed = (
        target[:, None] == jnp.arange(expert_total * capacity, dtype=jnp.int32)[None, :]
    ).astype(jnp.float32)
    placed = placed.reshape(token_count, top_count, expert_total * capacity)
    dispatch = jnp.sum(placed, axis=1).astype(jnp.bfloat16)
    lifted = jax.nn.sigmoid(scores)
    route_weight = 2.5 * lifted / jnp.sum(lifted, axis=-1, keepdims=True)
    combine = jnp.sum(placed * route_weight[:, :, None], axis=1)
    outgoing = lax.dot_general(
        dispatch, tokens, (((0,), (0,)), ((), ())), preferred_element_type=jnp.float32
    )
    outgoing = outgoing.astype(jnp.bfloat16).reshape(
        owner_count, local_experts, capacity, half_width
    )
    paired = jnp.stack(
        [
            gate_weight.reshape(local_experts, half_width, side_count, share_hidden),
            up_weight.reshape(local_experts, half_width, side_count, share_hidden),
        ],
        axis=3,
    )
    paired = paired.reshape(local_experts, half_width, 2 * local_hidden)
    widened = lax.all_gather(
        outgoing.reshape(owner_count, 1, local_experts, capacity, half_width),
        "grp",
        axis=1,
        tiled=True,
    )
    arrived = lax.all_to_all(widened, "ex", split_axis=0, concat_axis=0, tiled=True)
    ordered = jnp.transpose(arrived, (1, 0, 2, 3, 4)).reshape(
        rows_total, local_experts, capacity, half_width
    )
    partial_sums = jnp.einsum("secd,edh->sech", ordered, paired, preferred_element_type=jnp.float32)
    out_width = down_weight.shape[2]
    summed = lax.psum(partial_sums, "side")
    parts = summed.reshape(rows_total, local_experts, capacity, side_count, 2, share_hidden)
    hidden = (jax.nn.silu(parts[..., 0, :]) * parts[..., 1, :]).reshape(
        rows_total, local_experts, capacity, local_hidden
    )
    hidden = hidden.astype(jnp.bfloat16)
    expert_sum = make_fold(down_weight, lax.all_gather(hidden, "grp", axis=3, tiled=True))
    expert_out = expert_sum.astype(jnp.bfloat16).reshape(
        group_count, owner_count, local_experts, capacity, out_width
    )
    by_owner = lax.all_to_all(
        lax.all_to_all(expert_out, "grp", split_axis=0, concat_axis=4, tiled=True),
        "ex",
        split_axis=1,
        concat_axis=1,
        tiled=True,
    )
    returned = by_owner.reshape(expert_total * capacity, half_width).astype(jnp.float32)
    combined = jnp.dot(
        combine, returned, precision=lax.Precision.HIGHEST, preferred_element_type=jnp.float32
    )
    return combined.astype(jnp.bfloat16)


def solution(mesh):
    in_specs = (
        P(("grp", "ex"), "side"),
        P(("grp", "ex"), None),
        P(("grp", "ex"), None),
        P("ex", "side", "grp"),
        P("ex", "side", "grp"),
        P("ex", None, ("side", "grp")),
    )
    out_specs = P(("grp", "ex"), "side")
    return jax.shard_map(
        per_device, mesh=mesh, in_specs=in_specs, out_specs=out_specs, check_vma=False
    )
```

profile of v0, /device:TPU:0, one launch (start us, length us, event | category | flops | bytes accessed | tf_op | source)
XLA Modules:
  0.0 386.5 jit_solution(6132470382237630962)
XLA Ops:
  6.5 0.8 eq.29
  7.3 0.8 fusion.15
  8.1 0.8 multiply_divide_fusion
  9.3 0.7 multiply_add_fusion
  10.6 0.9 copy.26
  11.5 81.6 %stack_reshape.8 = bf16[4,3584,2,1,256]{4,3,2,1,0:T(2,128)(2,1)} reshape(bf16[4,3584,512]{2,1,0:T(8,128)(2,1)} %param.9) | data formatting | bytes 29360128 | tf_op jit(solution)/shard_map/stack;reshape | solution.py:45
  93.1 81.6 %stack_reshape.9 = bf16[4,3584,2,1,256]{4,3,2,1,0:T(2,128)(2,1)} reshape(bf16[4,3584,512]{2,1,0:T(8,128)(2,1)} %param.10) | data formatting | bytes 29360128 | tf_op jit(solution)/shard_map/stack;reshape | solution.py:45
  174.7 2.9 copy.27
  177.6 6.3 %all-to-all-start = ((bf16[4,4,4,3,3584]{4,2,3,1,0:T(4,128)(2,1)}), bf16[4,4,4,3,3584]{4,2,3,1,0:T(4,128)(2,1)S(1)}, u32[]{:S(2)}, u32[]{:S(2)}) async-start(bf16[4,4,4,3,3584]{4,2,3,1,0:T(4,128)(2,1)} %copy.27), calls=%async_computation | async-start | bytes 2752512 | tf_op jit(solution)/shard_map/all_to_all | solution.py:59
  183.9 64.5 %pad_maximum_fusion = bf16[4,3584,2,2,256]{4,3,2,1,0:T(2,128)(2,1)} fusion(bf16[4,3584,2,1,256]{4,3,2,1,0:T(2,128)(2,1)} %stack_reshape.9, bf16[4,3584,2,1,256]{4,3,2,1,0:T(2,128)(2,1)} %stack_reshape.8), kind=kLoop, calls=%fused_computation | loop fusion | flops 58720256 | bytes 58720256 | tf_op jit(solution)/shard_map/stack | solution.py:45
  248.5 47.1 %reshape.44 = bf16[4,3584,1024,1]{2,1,0,3:T(8,128)(2,1)} reshape(bf16[4,3584,2,2,256]{4,3,2,1,0:T(2,128)(2,1)} %pad_maximum_fusion) | data formatting | bytes 58720256 | tf_op jit(solution)/shard_map/reshape | solution.py:52
  295.6 1.1 copy.28
  296.6 0.4 reshape.40
  297.0 12.0 %fusion.4 = f32[16,4,3,1024]{3,0,2,1:T(8,128)S(1)} fusion(bf16[16,4,3,3584]{3,0,2,1:T(8,128)(2,1)S(1)} %reshape.40, bf16[4,3584,1024,1]{2,1,0,3:T(8,128)(2,1)} %reshape.44), kind=kOutput, calls=%fused_computation.7 | convolution fusion | flops 1409286144 | bytes 31522816 | tf_op jit(solution)/shard_map/secd,edh->sech/dot_general | solution.py:63
  309.1 1.6 reshape.41
  310.7 20.8 %all-reduce.2.cloned.1.call-done = f32[16,4,3,2,2,256]{5,4,3,0,2,1:T(2,128)} async-done(((f32[16,4,3,2,2,256]{5,4,3,0,2,1:T(2,128)}), f32[16,4,3,2,2,256]{5,4,3,0,2,1:T(2,128)}) %all-reduce.2.cloned.1.call-update) | async-done | bytes 786448 | tf_op jit(solution)/shard_map/psum | solution.py:65
  331.5 3.9 %slice_reduce_fusion.1 = (f32[16,4,3,2,256]{4,3,0,2,1:T(2,128)S(1)}, f32[16,4,3,2,256]{4,3,0,2,1:T(2,128)S(1)}) fusion(f32[16,4,3,2,2,256]{5,4,3,0,2,1:T(2,128)} %all-reduce.2.cloned.1.call-done), kind=kLoop, calls=%fused_computation.11 | loop fusion | bytes 1572864 | tf_op jit(solution)/shard_map/slice | solution.py:67
  335.4 0.3 squeeze.6
  335.7 0.3 squeeze.7
  336.2 12.8 %all_gather.7 = bf16[16,4,3,2048]{3,0,2,1:T(8,128)(2,1)S(1)} all-gather(bf16[16,4,3,512]{3,0,2,1:T(8,128)(2,1)S(1)} %multiply_convert_fusion), channel_id=1, replica_groups=mesh['side'=2,'grp'=4,'ex'=4] {'grp'}, dimensions={3}, use_global_device_ids=true | all-gather | bytes 983040 | tf_op jit(solution)/shard_map/all_gather | solution.py:71
  349.0 7.5 %fusion.10 = bf16[16,4,3,896]{3,0,2,1:T(8,128)(2,1)S(1)} fusion(bf16[16,4,3,2048]{3,0,2,1:T(8,128)(2,1)S(1)} %all_gather.7, bf16[4,2048,896]{2,1,0:T(8,128)(2,1)} %param.11), kind=kOutput, calls=%fused_computation.9 | convolution fusion | flops 704815104 | bytes 15810560 | tf_op jit(solution)/shard_map/sech,ehd->secd/dot_general | solution.py:8
  356.6 8.8 %all_to_all.28 = bf16[4,4,4,3,896]{4,2,3,1,0:T(4,128)(2,1)S(1)} all-to-all(bf16[4,4,4,3,896]{4,2,3,1,0:T(4,128)(2,1)S(1)} %bitcast.44), channel_id=1, replica_groups=mesh['side'=2,'grp'=4,'ex'=4] {'grp'}, dimensions={0} | all-to-all | bytes 688128 | tf_op jit(solution)/shard_map/all_to_all | solution.py:76
  365.5 12.8 %all_to_all.29 = bf16[1,4,4,3,3584]{4,2,3,0,1:T(4,128)(2,1)S(1)} all-to-all(bf16[1,4,4,3,3584]{4,2,3,0,1:T(4,128)(2,1)S(1)} %bitcast.46), channel_id=1, replica_groups=mesh['side'=2,'grp'=4,'ex'=4] {'ex'}, dimensions={1} | all-to-all | bytes 688128 | tf_op jit(solution)/shard_map/all_to_all | solution.py:75
  378.8 0.9 convolution_convert_fusion.1
  (22 shorter events, 1.9 us)
Async XLA Ops:
  6.5 3.5 copy-start
  6.5 168.2 %all-gather.2.cloned.1.call-start = ((), (), s32[]{:S(2)}) async-start(), calls=%async_computation.3 | async-start | bytes 1720320 | tf_op jit(solution)/shard_map/all_gather | solution.py:53
  177.6 117.9 %all-to-all-start = ((bf16[4,4,4,3,3584]{4,2,3,1,0:T(4,128)(2,1)}), bf16[4,4,4,3,3584]{4,2,3,1,0:T(4,128)(2,1)S(1)}, u32[]{:S(2)}, u32[]{:S(2)}) async-start(bf16[4,4,4,3,3584]{4,2,3,1,0:T(4,128)(2,1)} %copy.27), calls=%async_computation | async-start | bytes 2752512 | tf_op jit(solution)/shard_map/all_to_all | solution.py:59
  183.9 147.5 %all-reduce.2.cloned.1.call-start = ((), (), s32[]{:S(2)}) async-start(), calls=%async_computation.4 | async-start | bytes 1572864 | tf_op jit(solution)/shard_map/psum | solution.py:65
  296.6 83.0 %copy-start.1 = (bf16[3,3584]{1,0:T(4,128)(2,1)S(1)}, bf16[3,3584]{1,0:T(4,128)(2,1)}, u32[]{:S(2)}) copy-start(bf16[3,3584]{1,0:T(4,128)(2,1)} %param.6) | copy-start | bytes 64516
Sparse Core Ops, SparseCore 0:
  11.6 32.0 all-gather.1
  310.8 20.6 all-reduce.1
where the time goes:
time: 393 us; the launch traced here: 386 us
  local copies, waits for them, and re-layouts  223 us (57%)
  other arithmetic  67.3 us (17%)
  blocking collectives  34.4 us (9%)
  waiting for transfers between devices  20.9 us (5%)
  matrix products  20.7 us (5%)
  between operations  13.5 us (3%)
  starting transfers between devices  6.33 us (2%)
    another operation x2, local copies, waits for them, and re-layouts, per_device(): jnp.stack([gate_weight.reshape(local_experts, half_width, side_count, sha...  163 us
    another operation x1, other arithmetic, per_device(): jnp.stack([gate_weight.reshape(local_experts, half_width, side_count, sha...  64.5 us
    reshape x1, local copies, waits for them, and re-layouts, per_device(): paired = paired.reshape(local_experts, half_width, 2 * local_hidden)  47.1 us
    psum x1, waiting for transfers between devices, per_device(): summed = lax.psum(partial_sums, 'side')  20.8 us
    all_gather x1, blocking collectives, per_device(): lax.all_gather(hidden, 'grp', axis=3, tiled=True)  12.8 us
    all_to_all x1, blocking collectives, per_device(): lax.all_to_all(lax.all_to_all(expert_out, 'grp', split_axis=0, concat_axi...  12.8 us
    dot_general x1, matrix products, per_device(): jnp.einsum('secd,edh->sech', ordered, paired, preferred_element_type=jnp....  12 us
    all_to_all x1, blocking collectives, per_device(): lax.all_to_all(expert_out, 'grp', split_axis=0, concat_axis=4, tiled=True)  8.84 us
  transfers between devices with their start and end apart: 3, of which 1 were waited for; matrix products, arithmetic and copies ran while one was open for 71% of the time, Pallas kernels for 0%

commit v1 on v0

--- a/solution.py
+++ b/solution.py
@@ -1,7 +1,15 @@
+import functools
+
 import jax
 import jax.numpy as jnp
 from jax import lax
+from jax.experimental import pallas as pl
+from jax.experimental.pallas import tpu as pltpu
 from jax.sharding import PartitionSpec as P
+
+TOK = 3
+ROWS = 16
+PACK = ROWS // TOK
 
 
 def make_fold(table, piece):
@@ -86,6 +94,331 @@
     return combined.astype(jnp.bfloat16)
 
 
+def unpack_matrix(piece, tokens, rows, transposed=False):
+    shape = (rows, tokens) if transposed else (tokens, rows)
+    token = lax.broadcasted_iota(jnp.int32, shape, 1 if transposed else 0)
+    row = lax.broadcasted_iota(jnp.int32, shape, 0 if transposed else 1)
+    source = lax.shift_right_logical(token * 171, 9)
+    target = (ROWS - TOK) * source + token + TOK * piece
+    return jnp.where(row == target, 1.0, 0.0).astype(jnp.bfloat16)
+
+
+def fused_kernel(
+    dims,
+    tok_ref,
+    ids_ref,
+    score_ref,
+    gate_hbm,
+    up_hbm,
+    down_hbm,
+    out_ref,
+    gate_v,
+    up_v,
+    down_v,
+    pack_f,
+    block,
+    gathered,
+    x_ref,
+    mine,
+    other,
+    hidden,
+    acc,
+    ret,
+    back,
+    fin,
+    gate_sem,
+    up_sem,
+    down_sem,
+    tok_send,
+    tok_recv,
+    side_send,
+    side_recv,
+    hid_send,
+    hid_recv,
+    ret_send,
+    ret_recv,
+):
+    groups, owners, experts, width, hid, out_w, lanes, ret_lanes = dims
+    count = groups * owners
+    tokens = count * TOK
+    rows = count * ROWS
+    side = lax.axis_index("side")
+    grp = lax.axis_index("grp")
+    own = lax.axis_index("ex")
+    me = grp * owners + own
+    sibling = {"side": 1 - side}
+
+    def loads(e):
+        return (
+            pltpu.make_async_copy(gate_hbm.at[e], gate_v.at[e], gate_sem.at[e]),
+            pltpu.make_async_copy(up_hbm.at[e], up_v.at[e], up_sem.at[e]),
+            pltpu.make_async_copy(down_hbm.at[e], down_v.at[e], down_sem.at[e]),
+        )
+
+    for e in range(experts):
+        gate_copy, up_copy, _ = loads(e)
+        gate_copy.start()
+        up_copy.start()
+    for e in range(experts):
+        loads(e)[2].start()
+
+    def peer(step):
+        target = lax.rem(me + step, count)
+        return target, {"grp": target // owners, "ex": lax.rem(target, owners)}
+
+    barrier = pltpu.get_barrier_semaphore()
+    for step in range(1, count):
+        pl.semaphore_signal(
+            barrier, inc=1, device_id=peer(step)[1], device_id_type=pl.DeviceIdType.MESH
+        )
+    pl.semaphore_signal(barrier, inc=1, device_id=sibling, device_id_type=pl.DeviceIdType.MESH)
+
+    lifted = jax.nn.sigmoid(score_ref[...])
+    route = 2.5 * lifted / jnp.sum(lifted, axis=-1, keepdims=True)
+    ids = ids_ref[...]
+    expert_lane = lax.broadcasted_iota(jnp.int32, (TOK, 128), 1)
+    dense = jnp.zeros((TOK, 128), jnp.float32)
+    for k in range(ids.shape[1]):
+        dense = dense + jnp.where(ids[:, k : k + 1] == expert_lane, route[:, k : k + 1], 0.0)
+    high = dense.astype(jnp.bfloat16).astype(jnp.float32)
+    low = dense - high
+    pack_f[...] = jnp.zeros_like(pack_f)
+    for piece in range(PACK):
+        begin = piece * lanes
+        size = min(lanes, width - begin)
+        pack_f[pl.ds(TOK * piece, TOK), pl.ds(0, size)] = tok_ref[:, pl.ds(begin, size)].astype(
+            jnp.float32
+        )
+    spare = width - (PACK - 1) * lanes
+    pack_f[pl.ds(TOK * (PACK - 1), TOK), pl.ds(spare, 128)] = high
+    pack_f[pl.ds(TOK * (PACK - 1), TOK), pl.ds(spare + 128, 128)] = low
+    packed = pack_f[...].astype(jnp.bfloat16)
+    block[...] = packed
+    my_rows = pl.ds(pl.multiple_of(me * ROWS, ROWS), ROWS)
+    gathered[my_rows, :] = packed
+
+    pl.semaphore_wait(barrier, count)
+
+    def token_copy(step):
+        return pltpu.make_async_remote_copy(
+            src_ref=block,
+            dst_ref=gathered.at[my_rows],
+            send_sem=tok_send.at[step - 1],
+            recv_sem=tok_recv.at[step - 1],
+            device_id=peer(step)[1],
+            device_id_type=pl.DeviceIdType.MESH,
+        )
+
+    token_copies = [token_copy(step) for step in range(1, count)]
+    for copy in token_copies:
+        copy.start()
+    for copy in token_copies:
+        copy.wait_recv()
+
+    weights = None
+    for piece in range(PACK):
+        part = jnp.dot(
+            unpack_matrix(piece, tokens, rows),
+            gathered[...],
+            preferred_element_type=jnp.float32,
+        )
+        size = min(lanes, width - piece * lanes)
+        x_ref[:, pl.ds(piece * lanes, size)] = part[:, :size].astype(jnp.bfloat16)
+        if piece == PACK - 1:
+            weights = part[:, spare : spare + 128] + part[:, spare + 128 : spare + 256]
+
+    def side_copy(e):
+        return pltpu.make_async_remote_copy(
+            src_ref=mine.at[e],
+            dst_ref=other.at[e],
+            send_sem=side_send.at[e],
+            recv_sem=side_recv.at[e],
+            device_id=sibling,
+            device_id_type=pl.DeviceIdType.MESH,
+        )
+
+    def hidden_copy(e, step):
+        return pltpu.make_async_remote_copy(
+            src_ref=hidden.at[e, grp],
+            dst_ref=hidden.at[e, grp],
+            send_sem=hid_send.at[e, step - 1],
+            recv_sem=hid_recv.at[e, step - 1],
+            device_id={"grp": lax.rem(grp + step, groups)},
+            device_id_type=pl.DeviceIdType.MESH,
+        )
+
+    def gate_up(e):
+        gate_copy, up_copy, _ = loads(e)
+        for weight, copy, begin in ((gate_v, gate_copy, 0), (up_v, up_copy, hid)):
+            copy.wait()
+            mine[e, :, pl.ds(begin, hid)] = jnp.dot(
+                x_ref[...], weight[e], preferred_element_type=jnp.float32
+            )
+        side_copy(e).start()
+
+    def activate(e):
+        side_copy(e).wait_recv()
+        gate = mine[e, :, pl.ds(0, hid)] + other[e, :, pl.ds(0, hid)]
+        up = mine[e, :, pl.ds(hid, hid)] + other[e, :, pl.ds(hid, hid)]
+        hidden[e, grp] = (gate / (1.0 + jnp.exp(-gate)) * up).astype(jnp.bfloat16)
+        for step in range(1, groups):
+            hidden_copy(e, step).start()
+
+    acc[...] = jnp.zeros_like(acc)
+
+    def down(e):
+        loads(e)[2].wait()
+        for step in range(1, groups):
+            hidden_copy(e, step).wait_recv()
+        lhs = jnp.concatenate([hidden[e, j] for j in range(groups)], axis=1)
+        lane = lax.broadcasted_iota(jnp.int32, weights.shape, 1)
+        factor = jnp.sum(
+            jnp.where(lane == own * experts + e, weights, 0.0), axis=1, keepdims=True
+        )
+        for begin in range(0, out_w, 256):
+            size = min(256, out_w - begin)
+            result = jnp.dot(
+                lhs, down_v[e, :, pl.ds(begin, size)], preferred_element_type=jnp.float32
+            )
+            result = result.astype(jnp.bfloat16).astype(jnp.float32)
+            acc[:, pl.ds(begin, size)] += factor * result
+
+    for e in range(experts):
+        gate_up(e)
+        if e > 0:
+            activate(e - 1)
+    if experts > 1:
+        down(0)
+    activate(experts - 1)
+    for e in range(1 if experts > 1 else 0, experts):
+        down(e)
+
+    packed_out = jnp.zeros((rows, ret_lanes), jnp.float32)
+    for piece in range(acc.shape[1] // ret_lanes):
+        packed_out = packed_out + jnp.dot(
+            unpack_matrix(piece, tokens, rows, True),
+            acc[:, pl.ds(piece * ret_lanes, ret_lanes)].astype(jnp.bfloat16),
+            preferred_element_type=jnp.float32,
+        )
+    ret[...] = packed_out.astype(jnp.bfloat16)
+
+    def return_copy(step):
+        target, device = peer(step)
+        return pltpu.make_async_remote_copy(
+            src_ref=ret.at[pl.ds(pl.multiple_of(target * ROWS, ROWS), ROWS)],
+            dst_ref=back.at[my_rows],
+            send_sem=ret_send.at[step - 1],
+            recv_sem=ret_recv.at[step - 1],
+            device_id=device,
+            device_id_type=pl.DeviceIdType.MESH,
+        )
+
+    return_copies = [return_copy(step) for step in range(1, count)]
+    for copy in return_copies:
+        copy.start()
+    back[my_rows, :] = ret[my_rows, :]
+    for copy in token_copies:
+        copy.wait_send()
+    for e in range(experts):
+        side_copy(e).wait_send()
+        for step in range(1, groups):
+            hidden_copy(e, step).wait_send()
+    for copy in return_copies:
+        copy.wait_recv()
+    for j in range(groups):
+        total = back[pl.ds(j * owners * ROWS, ROWS), :].astype(jnp.float32)
+        for k in range(1, owners):
+            total = total + back[pl.ds((j * owners + k) * ROWS, ROWS), :].astype(jnp.float32)
+        fin[j] = total
+        for piece in range(acc.shape[1] // ret_lanes):
+            begin = piece * ret_lanes
+            size = min(ret_lanes, out_w - begin)
+            out_ref[:, pl.ds(j * out_w + begin, size)] = fin[
+                j, pl.ds(TOK * piece, TOK), pl.ds(0, size)
+            ].astype(jnp.bfloat16)
+    for copy in return_copies:
+        copy.wait_send()
+
+
+def ceil_lanes(size, pieces):
+    return -(-size // (128 * pieces)) * 128
+
+
+def fused(dims, tokens, expert_ids, scores, gate_weight, up_weight, down_weight):
+    groups, owners, experts, width, hid, out_w, lanes, ret_lanes = dims
+    count = groups * owners
+    acc_w = -(-out_w // ret_lanes) * ret_lanes
+    rows = count * ROWS
+    vmem = pl.BlockSpec(memory_space=pltpu.VMEM)
+    hbm = pl.BlockSpec(memory_space=pl.ANY)
+    dma = pltpu.SemaphoreType.DMA
+    weight_count = gate_weight.size + up_weight.size + down_weight.size
+    return pl.pallas_call(
+        functools.partial(fused_kernel, dims),
+        out_shape=jax.ShapeDtypeStruct(tokens.shape, jnp.bfloat16),
+        in_specs=[vmem, vmem, vmem, hbm, hbm, hbm],
+        out_specs=vmem,
+        scratch_shapes=[
+            pltpu.VMEM(gate_weight.shape, jnp.bfloat16),
+            pltpu.VMEM(up_weight.shape, jnp.bfloat16),
+            pltpu.VMEM(down_weight.shape, jnp.bfloat16),
+            pltpu.VMEM((ROWS, lanes), jnp.float32),
+            pltpu.VMEM((ROWS, lanes), jnp.bfloat16),
+            pltpu.VMEM((rows, lanes), jnp.bfloat16),
+            pltpu.VMEM((count * TOK, width), jnp.bfloat16),
+            pltpu.VMEM((experts, count * TOK, 2 * hid), jnp.float32),
+            pltpu.VMEM((experts, count * TOK, 2 * hid), jnp.float32),
+            pltpu.VMEM((experts, groups, count * TOK, hid), jnp.bfloat16),
+            pltpu.VMEM((count * TOK, acc_w), jnp.float32),
+            pltpu.VMEM((rows, ret_lanes), jnp.bfloat16),
+            pltpu.VMEM((rows, ret_lanes), jnp.bfloat16),
+            pltpu.VMEM((groups, ROWS, ret_lanes), jnp.float32),
+            dma((experts,)),
+            dma((experts,)),
+            dma((experts,)),
+            dma((count - 1,)),
+            dma((count - 1,)),
+            dma((experts,)),
+            dma((experts,)),
+            dma((experts, groups - 1)),
+            dma((experts, groups - 1)),
+            dma((count - 1,)),
+            dma((count - 1,)),
+        ],
+        compiler_params=pltpu.CompilerParams(
+            collective_id=0, has_side_effects=True, vmem_limit_bytes=58 * 1024 * 1024
+        ),
+        cost_estimate=pl.CostEstimate(
+            flops=2 * count * TOK * weight_count,
+            bytes_accessed=2 * weight_count,
+            transcendentals=count * TOK * experts * hid,
+        ),
+    )(tokens, expert_ids, scores, gate_weight, up_weight, down_weight)
+
+
+def choose(tokens, expert_ids, scores, gate_weight, up_weight, down_weight):
+    groups, owners = lax.axis_size("grp"), lax.axis_size("ex")
+    experts, width, hid = gate_weight.shape
+    out_w = down_weight.shape[2]
+    lanes = ceil_lanes(width + 256, PACK)
+    ret_lanes = ceil_lanes(out_w, PACK)
+    fits = (
+        tokens.shape[0] == TOK
+        and lax.axis_size("side") == 2
+        and groups > 1
+        and groups * owners == 16
+        and hid % 128 == 0
+        and out_w % 128 == 0
+        and width - (PACK - 1) * lanes > 0
+        and experts * owners <= 128
+        and experts * (2 * width * hid + groups * hid * out_w) * 2 <= 44 * 1024 * 1024
+    )
+    if not fits:
+        return per_device(tokens, expert_ids, scores, gate_weight, up_weight, down_weight)
+    dims = (groups, owners, experts, width, hid, out_w, lanes, ret_lanes)
+    return fused(dims, tokens, expert_ids, scores, gate_weight, up_weight, down_weight)
+
+
 def solution(mesh):
     in_specs = (
         P(("grp", "ex"), "side"),
@@ -97,5 +430,5 @@
     )
     out_specs = P(("grp", "ex"), "side")
     return jax.shard_map(
-        per_device, mesh=mesh, in_specs=in_specs, out_specs=out_specs, check_vma=False
-    )
+        choose, mesh=mesh, in_specs=in_specs, out_specs=out_specs, check_vma=False
+    )

time: 393 us -> 41.1 us (0.10); the launches traced: 386 us -> 40.8 us
  local copies, waits for them, and re-layouts: 223 us -> 1.37 us
  other arithmetic: 67.3 us -> 0 us
  Pallas kernels: 0 us -> 39.4 us
  blocking collectives: 34.4 us -> 0 us
  waiting for transfers between devices: 20.9 us -> 0 us
  matrix products: 20.7 us -> 0 us
  between operations: 13.5 us -> 0.01 us
  starting transfers between devices: 6.33 us -> 0 us
    another operation x4 -> x0, local copies, waits for them, and re-layouts: 164 us -> none  [the longest x2 163 us: per_device(): jnp.stack([gate_weight.reshape(local_experts, half_width, side_count, sha...]
    another operation x2 -> x0, other arithmetic: 64.6 us -> none  [the longest x1 64.5 us: per_device(): jnp.stack([gate_weight.reshape(local_experts, half_width, side_count, sha...]
    reshape x5 -> x0, local copies, waits for them, and re-layouts: 49.4 us -> none  [the longest x1 47.1 us: per_device(): paired = paired.reshape(local_experts, half_width, 2 * local_hidden)]
    pallas_call x0 -> x1, Pallas kernels: none -> 39.4 us  [fused(): pl.pallas_call(functools.partial(fused_kernel, dims), out_shape=jax.Shape...]
    all_to_all x2 -> x0, blocking collectives: 21.6 us -> none  [the longest x1 12.8 us: per_device(): lax.all_to_all(lax.all_to_all(expert_out, 'grp', split_axis=0, concat_axi...]
    psum x1 -> x0, waiting for transfers between devices: 20.8 us -> none  [per_device(): summed = lax.psum(partial_sums, 'side')]
    dot_general x4 -> x0, matrix products: 20.7 us -> none  [the longest x1 12 us: per_device(): jnp.einsum('secd,edh->sech', ordered, paired, preferred_element_type=jnp....]
    all_gather x1 -> x0, blocking collectives: 12.8 us -> none  [per_device(): lax.all_gather(hidden, 'grp', axis=3, tiled=True)]
  transfers between devices with their start and end apart: 3 -> 0, of which waited for: 1 -> 0; matrix products, arithmetic and copies ran while one was open for 71% -> 0% of each run, Pallas kernels for 0% -> 0%
where the time goes in v1:
time: 41.1 us; the launch traced here: 40.8 us
  Pallas kernels  39.4 us (96%)
  local copies, waits for them, and re-layouts  1.37 us (3%)
    pallas_call x1, Pallas kernels, fused(): pl.pallas_call(functools.partial(fused_kernel, dims), out_shape=jax.Shape...  39.4 us
    unnamed x1, local copies, waits for them, and re-layouts  1.37 us

profile of v1, /device:TPU:0, one launch (start us, length us, event | category | flops | bytes accessed | tf_op | source)
XLA Modules:
  0.0 40.8 jit_solution(13556560202135564578)
XLA Ops:
  0.0 39.4 %shard_map.64 = bf16[3,3584]{1,0:T(4,128)(2,1)} custom-call(bf16[3,3584]{1,0:T(4,128)(2,1)} %tok_ref.1, s32[3,8]{1,0:T(4,128)} %ids_ref.1, f32[3,8]{1,0:T(4,128)} %score_ref.1, bf16[4,3584,512]{2,1,0:T(8,128)(2,1)} %gate_hbm.1, bf16[4,3584,512]{2,1,0:T(8,128)(2,1)} %up_hbm.1, bf16[4,2048,896]{2,1,0:T(8,128)(2,1)} %down_hbm.1), custom_call_target="tpu_custom_call" | custom-call | flops 2113929216 | bytes 44040192 | tf_op jit(solution)/shard_map/pallas_call | solution.py:356
  39.5 1.4 %copy.8 = bf16[3,3584]{1,0:T(4,128)(2,1)} copy(bf16[3,3584]{1,0:T(4,128)(2,1)} %shard_map.64) | data formatting | bytes 43008

commit v2 on v1

v2 whole, which is shorter than its diff:
```python
import functools

import jax
import jax.numpy as jnp
from jax import lax
from jax.experimental import pallas as pl
from jax.experimental.pallas import tpu as pltpu
from jax.sharding import PartitionSpec as P

TOK = 3
ROWS = 16
PACK = ROWS // TOK


def make_fold(table, piece):
    return jnp.einsum("sech,ehd->secd", piece, table, preferred_element_type=jnp.float32)


def per_device(tokens, expert_ids, scores, gate_weight, up_weight, down_weight):
    side_count = lax.axis_size("side")
    group_count = lax.axis_size("grp")
    owner_count = lax.axis_size("ex")
    local_experts = gate_weight.shape[0]
    expert_total = local_experts * owner_count
    capacity = tokens.shape[0]
    token_count = tokens.shape[0]
    top_count = expert_ids.shape[1]
    half_width = tokens.shape[1]
    local_hidden = gate_weight.shape[2]
    share_hidden = local_hidden // side_count
    rows_total = group_count * owner_count
    flat_ids = expert_ids.reshape(-1)
    onehot = (flat_ids[:, None] == jnp.arange(expert_total, dtype=jnp.int32)[None, :]).astype(
        jnp.int32
    )
    earlier = jnp.cumsum(onehot, axis=0) - onehot
    slot_of = jnp.sum(earlier * onehot, axis=1)
    target = flat_ids * capacity + slot_of
    placed = (
        target[:, None] == jnp.arange(expert_total * capacity, dtype=jnp.int32)[None, :]
    ).astype(jnp.float32)
    placed = placed.reshape(token_count, top_count, expert_total * capacity)
    dispatch = jnp.sum(placed, axis=1).astype(jnp.bfloat16)
    lifted = jax.nn.sigmoid(scores)
    route_weight = 2.5 * lifted / jnp.sum(lifted, axis=-1, keepdims=True)
    combine = jnp.sum(placed * route_weight[:, :, None], axis=1)
    outgoing = lax.dot_general(
        dispatch, tokens, (((0,), (0,)), ((), ())), preferred_element_type=jnp.float32
    )
    outgoing = outgoing.astype(jnp.bfloat16).reshape(
        owner_count, local_experts, capacity, half_width
    )
    paired = jnp.stack(
        [
            gate_weight.reshape(local_experts, half_width, side_count, share_hidden),
            up_weight.reshape(local_experts, half_width, side_count, share_hidden),
        ],
        axis=3,
    )
    paired = paired.reshape(local_experts, half_width, 2 * local_hidden)
    widened = lax.all_gather(
        outgoing.reshape(owner_count, 1, local_experts, capacity, half_width),
        "grp",
        axis=1,
        tiled=True,
    )
    arrived = lax.all_to_all(widened, "ex", split_axis=0, concat_axis=0, tiled=True)
    ordered = jnp.transpose(arrived, (1, 0, 2, 3, 4)).reshape(
        rows_total, local_experts, capacity, half_width
    )
    partial_sums = jnp.einsum("secd,edh->sech", ordered, paired, preferred_element_type=jnp.float32)
    out_width = down_weight.shape[2]
    summed = lax.psum(partial_sums, "side")
    parts = summed.reshape(rows_total, local_experts, capacity, side_count, 2, share_hidden)
    hidden = (jax.nn.silu(parts[..., 0, :]) * parts[..., 1, :]).reshape(
        rows_total, local_experts, capacity, local_hidden
    )
    hidden = hidden.astype(jnp.bfloat16)
    expert_sum = make_fold(down_weight, lax.all_gather(hidden, "grp", axis=3, tiled=True))
    expert_out = expert_sum.astype(jnp.bfloat16).reshape(
        group_count, owner_count, local_experts, capacity, out_width
    )
    by_owner = lax.all_to_all(
        lax.all_to_all(expert_out, "grp", split_axis=0, concat_axis=4, tiled=True),
        "ex",
        split_axis=1,
        concat_axis=1,
        tiled=True,
    )
    returned = by_owner.reshape(expert_total * capacity, half_width).astype(jnp.float32)
    combined = jnp.dot(
        combine, returned, precision=lax.Precision.HIGHEST, preferred_element_type=jnp.float32
    )
    return combined.astype(jnp.bfloat16)


def unpack_matrix(piece, tokens, rows, transposed=False):
    shape = (rows, tokens) if transposed else (tokens, rows)
    token = lax.broadcasted_iota(jnp.int32, shape, 1 if transposed else 0)
    row = lax.broadcasted_iota(jnp.int32, shape, 0 if transposed else 1)
    source = lax.shift_right_logical(token * 171, 9)
    target = (ROWS - TOK) * source + token + TOK * piece
    return jnp.where(row == target, 1.0, 0.0).astype(jnp.bfloat16)


def fused_kernel(
    dims,
    tok_hbm,
    ids_hbm,
    score_hbm,
    gate_hbm,
    up_hbm,
    down_hbm,
    out_ref,
    tok_ref,
    ids_ref,
    score_ref,
    gate_v,
    up_v,
    down_v,
    pack_f,
    block,
    gathered,
    x_ref,
    mine,
    other,
    hidden,
    acc,
    ret,
    back,
    fin,
    in_sem,
    gate_sem,
    up_sem,
    down_sem,
    tok_send,
    tok_recv,
    side_send,
    side_recv,
    hid_send,
    hid_recv,
    ret_send,
    ret_recv,
):
    groups, owners, experts, width, hid, out_w, lanes = dims
    count = groups * owners
    tokens = count * TOK
    rows = count * ROWS
    span = PACK * lanes
    cut = span // 256 * 256
    early = min(2, experts)
    side = lax.axis_index("side")
    grp = lax.axis_index("grp")
    own = lax.axis_index("ex")
    me = grp * owners + own
    sibling = {"side": 1 - side}
    mesh_id = pl.DeviceIdType.MESH

    inputs = [
        pltpu.make_async_copy(source, target, in_sem.at[i])
        for i, (source, target) in enumerate(
            ((tok_hbm, tok_ref), (ids_hbm, ids_ref), (score_hbm, score_ref))
        )
    ]
    for copy in inputs:
        copy.start()

    def gate_up_loads(e, half):
        part = pl.ds(0, cut) if half == 0 else pl.ds(cut, width - cut)
        return (
            pltpu.make_async_copy(
                gate_hbm.at[e, part], gate_v.at[e, part], gate_sem.at[e, half]
            ),
            pltpu.make_async_copy(up_hbm.at[e, part], up_v.at[e, part], up_sem.at[e, half]),
        )

    def down_load(e):
        return pltpu.make_async_copy(down_hbm.at[e], down_v.at[e], down_sem.at[e])

    order = [(e, 0) for e in range(early)] + [(e, 1) for e in range(early)]
    order += [(e, half) for e in range(early, experts) for half in range(2)]
    for e, half in order:
        for copy in gate_up_loads(e, half):
            copy.start()
    for e in range(experts):
        down_load(e).start()

    def peer(step):
        target = lax.rem(me + step, count)
        return target, {"grp": target // owners, "ex": lax.rem(target, owners)}

    barrier = pltpu.get_barrier_semaphore()
    for step in range(1, count):
        pl.semaphore_signal(barrier, inc=1, device_id=peer(step)[1], device_id_type=mesh_id)
    pl.semaphore_signal(barrier, inc=1, device_id=sibling, device_id_type=mesh_id)

    pack_f[...] = jnp.zeros_like(pack_f)
    for copy in inputs:
        copy.wait()
    lifted = jax.nn.sigmoid(score_ref[...])
    route = 2.5 * lifted / jnp.sum(lifted, axis=-1, keepdims=True)
    ids = ids_ref[...]
    expert_lane = lax.broadcasted_iota(jnp.int32, (TOK, 128), 1)
    dense = jnp.zeros((TOK, 128), jnp.float32)
    for k in range(ids.shape[1]):
        dense = dense + jnp.where(ids[:, k : k + 1] == expert_lane, route[:, k : k + 1], 0.0)
    high = dense.astype(jnp.bfloat16).astype(jnp.float32)
    low = dense - high
    spare = width - (2 * PACK - 1) * lanes
    my_rows = pl.ds(pl.multiple_of(me * ROWS, ROWS), ROWS)
    for half in range(2):
        for piece in range(PACK):
            begin = half * span + piece * lanes
            size = min(lanes, width - begin)
            pack_f[half, pl.ds(TOK * piece, TOK), pl.ds(0, size)] = tok_ref[
                :, pl.ds(begin, size)
            ].astype(jnp.float32)
        if half == 1:
            last = pl.ds(TOK * (PACK - 1), TOK)
            pack_f[half, last, pl.ds(spare, 128)] = high
            pack_f[half, last, pl.ds(spare + 128, 128)] = low
        packed = pack_f[half].astype(jnp.bfloat16)
        block[half] = packed
        gathered[half, my_rows, :] = packed

    pl.semaphore_wait(barrier, count)

    def flip(bits):
        value = own
        for bit in (1, 2):
            if bits & bit:
                value = value + bit - 2 * bit * lax.rem(value // bit, 2)
        return value

    def token_copy(half, along_grp, along_ex):
        if along_grp and along_ex:
            start_row = (grp * owners + flip(along_ex)) * ROWS
            place = pl.ds(pl.multiple_of(start_row, ROWS), ROWS)
            source = gathered.at[half, place]
        else:
            place = my_rows
            source = block.at[half]
        device = (
            {"grp": lax.rem(grp + along_grp, groups)} if along_grp else {"ex": flip(along_ex)}
        )
        return pltpu.make_async_remote_copy(
            src_ref=source,
            dst_ref=gathered.at[half, place],
            send_sem=tok_send.at[half, along_grp, along_ex],
            recv_sem=tok_recv.at[half, along_grp, along_ex],
            device_id=device,
            device_id_type=mesh_id,
        )

    for half in range(2):
        for along_ex in range(1, owners):
            token_copy(half, 0, along_ex).start()
    for half in range(2):
        for along_grp in range(1, groups):
            token_copy(half, along_grp, 0).start()
        for along_ex in range(1, owners):
            token_copy(half, 0, along_ex).wait_recv()
            for along_grp in range(1, groups):
                token_copy(half, along_grp, along_ex).start()

    acc[...] = jnp.zeros_like(acc)
    picks = [unpack_matrix(piece, tokens, rows) for piece in range(PACK)]

    def unpack(half):
        for along_grp in range(1, groups):
            for along_ex in range(owners):
                token_copy(half, along_grp, along_ex).wait_recv()
        for piece in range(PACK):
            part = jnp.dot(picks[piece], gathered[half], preferred_element_type=jnp.float32)
            begin = half * span + piece * lanes
            size = min(lanes, width - begin)
            x_ref[:, pl.ds(begin, size)] = part[:, :size].astype(jnp.bfloat16)
        return part[:, spare : spare + 128] + part[:, spare + 128 : spare + 256]

    def side_copy(e):
        return pltpu.make_async_remote_copy(
            src_ref=mine.at[e],
            dst_ref=other.at[e],
            send_sem=side_send.at[e],
            recv_sem=side_recv.at[e],
            device_id=sibling,
            device_id_type=mesh_id,
        )

    def hidden_copy(e, step):
        return pltpu.make_async_remote_copy(
            src_ref=hidden.at[e, grp],
            dst_ref=hidden.at[e, grp],
            send_sem=hid_send.at[e, step - 1],
            recv_sem=hid_recv.at[e, step - 1],
            device_id={"grp": lax.rem(grp + step, groups)},
            device_id_type=mesh_id,
        )

    def gate_up_first(e):
        for i, weight in enumerate((gate_v, up_v)):
            gate_up_loads(e, 0)[i].wait()
            mine[e, :, pl.ds(i * hid, hid)] = jnp.dot(
                x_ref[:, pl.ds(0, cut)],
                weight[e, pl.ds(0, cut)],
                preferred_element_type=jnp.float32,
            )

    def gate_up_rest(e):
        for i, weight in enumerate((gate_v, up_v)):
            gate_up_loads(e, 1)[i].wait()
            if e < early:
                mine[e, :, pl.ds(i * hid, hid)] += jnp.dot(
                    x_ref[:, pl.ds(cut, width - cut)],
                    weight[e, pl.ds(cut, width - cut)],
                    preferred_element_type=jnp.float32,
                )
            else:
                gate_up_loads(e, 0)[i].wait()
                mine[e, :, pl.ds(i * hid, hid)] = jnp.dot(
                    x_ref[...], weight[e], preferred_element_type=jnp.float32
                )
        side_copy(e).start()

    def activate(e):
        side_copy(e).wait_recv()
        gate = mine[e, :, pl.ds(0, hid)] + other[e, :, pl.ds(0, hid)]
        up = mine[e, :, pl.ds(hid, hid)] + other[e, :, pl.ds(hid, hid)]
        hidden[e, grp] = (gate / (1.0 + jnp.exp(-gate)) * up).astype(jnp.bfloat16)
        for step in range(1, groups):
            hidden_copy(e, step).start()

    pieces = out_w // 128
    halves = ((0, -(-pieces // 2)), (-(-pieces // 2), pieces))

    def down(e, half):
        if half == 0:
            down_load(e).wait()
            for step in range(1, groups):
                hidden_copy(e, step).wait_recv()
        lhs = jnp.concatenate([hidden[e, j] for j in range(groups)], axis=1)
        lane = lax.broadcasted_iota(jnp.int32, weights.shape, 1)
        factor = jnp.sum(
            jnp.where(lane == own * experts + e, weights, 0.0), axis=1, keepdims=True
        )
        first, stop = halves[half]
        for begin in range(first * 128, stop * 128, 256):
            size = min(256, stop * 128 - begin)
            result = jnp.dot(
                lhs, down_v[e, :, pl.ds(begin, size)], preferred_element_type=jnp.float32
            )
            result = result.astype(jnp.bfloat16).astype(jnp.float32)
            acc[:, pl.ds(begin, size)] += factor * result

    def return_copy(half, step):
        target, device = peer(step)
        return pltpu.make_async_remote_copy(
            src_ref=ret.at[half, pl.ds(pl.multiple_of(target * ROWS, ROWS), ROWS)],
            dst_ref=back.at[half, my_rows],
            send_sem=ret_send.at[half, step - 1],
            recv_sem=ret_recv.at[half, step - 1],
            device_id=device,
            device_id_type=mesh_id,
        )

    def send_back(half):
        first, stop = halves[half]
        packed_out = jnp.zeros((rows, 128), jnp.float32)
        for piece in range(first, stop):
            packed_out = packed_out + jnp.dot(
                unpack_matrix(piece - first, tokens, rows, True),
                acc[:, pl.ds(piece * 128, 128)].astype(jnp.bfloat16),
                preferred_element_type=jnp.float32,
            )
        ret[half] = packed_out.astype(jnp.bfloat16)
        for step in range(1, count):
            return_copy(half, step).start()
        back[half, my_rows, :] = ret[half, my_rows, :]

    unpack(0)
    for e in range(early):
        gate_up_first(e)
    weights = unpack(1)
    for e in range(experts):
        gate_up_rest(e)
        if e > 0:
            activate(e - 1)
    if experts > 1:
        down(0, 0)
    activate(experts - 1)
    if experts > 1:
        down(0, 1)
    for e in range(1, experts - 1):
        down(e, 0)
    for e in range(1, experts - 2):
        down(e, 1)
    down(experts - 1, 0)
    send_back(0)
    for e in range(max(1, experts - 2), experts):
        down(e, 1)
    send_back(1)

    for half in range(2):
        for along_ex in range(1, owners):
            token_copy(half, 0, along_ex).wait_send()
        for along_grp in range(1, groups):
            for along_ex in range(owners):
                token_copy(half, along_grp, along_ex).wait_send()
    for e in range(experts):
        side_copy(e).wait_send()
        for step in range(1, groups):
            hidden_copy(e, step).wait_send()
    for half in range(2):
        for step in range(1, count):
            return_copy(half, step).wait_recv()
        first, stop = halves[half]
        for j in range(groups):
            total = back[half, pl.ds(j * owners * ROWS, ROWS), :].astype(jnp.float32)
            for k in range(1, owners):
                place = pl.ds((j * owners + k) * ROWS, ROWS)
                total = total + back[half, place, :].astype(jnp.float32)
            fin[half, j] = total
            for piece in range(first, stop):
                out_ref[:, pl.ds(j * out_w + piece * 128, 128)] = fin[
                    half, j, pl.ds(TOK * (piece - first), TOK), :
                ].astype(jnp.bfloat16)
    for half in range(2):
        for step in range(1, count):
            return_copy(half, step).wait_send()


def ceil_lanes(size, pieces):
    return -(-size // (128 * pieces)) * 128


def fused(dims, tokens, expert_ids, scores, gate_weight, up_weight, down_weight):
    groups, owners, experts, width, hid, out_w, lanes = dims
    count = groups * owners
    rows = count * ROWS
    vmem = pl.BlockSpec(memory_space=pltpu.VMEM)
    hbm = pl.BlockSpec(memory_space=pl.ANY)
    dma = pltpu.SemaphoreType.DMA
    weight_count = gate_weight.size + up_weight.size + down_weight.size
    return pl.pallas_call(
        functools.partial(fused_kernel, dims),
        out_shape=jax.ShapeDtypeStruct(tokens.shape, jnp.bfloat16),
        in_specs=[hbm] * 6,
        out_specs=vmem,
        scratch_shapes=[
            pltpu.VMEM(tokens.shape, jnp.bfloat16),
            pltpu.VMEM(expert_ids.shape, jnp.int32),
            pltpu.VMEM(scores.shape, jnp.float32),
            pltpu.VMEM(gate_weight.shape, jnp.bfloat16),
            pltpu.VMEM(up_weight.shape, jnp.bfloat16),
            pltpu.VMEM(down_weight.shape, jnp.bfloat16),
            pltpu.VMEM((2, ROWS, lanes), jnp.float32),
            pltpu.VMEM((2, ROWS, lanes), jnp.bfloat16),
            pltpu.VMEM((2, rows, lanes), jnp.bfloat16),
            pltpu.VMEM((count * TOK, width), jnp.bfloat16),
            pltpu.VMEM((experts, count * TOK, 2 * hid), jnp.float32),
            pltpu.VMEM((experts, count * TOK, 2 * hid), jnp.float32),
            pltpu.VMEM((experts, groups, count * TOK, hid), jnp.bfloat16),
            pltpu.VMEM((count * TOK, out_w), jnp.float32),
            pltpu.VMEM((2, rows, 128), jnp.bfloat16),
            pltpu.VMEM((2, rows, 128), jnp.bfloat16),
            pltpu.VMEM((2, groups, ROWS, 128), jnp.float32),
            dma((3,)),
            dma((experts, 2)),
            dma((experts, 2)),
            dma((experts,)),
            dma((2, groups, owners)),
            dma((2, groups, owners)),
            dma((experts,)),
            dma((experts,)),
            dma((experts, groups - 1)),
            dma((experts, groups - 1)),
            dma((2, count - 1)),
            dma((2, count - 1)),
        ],
        compiler_params=pltpu.CompilerParams(
            collective_id=0, has_side_effects=True, vmem_limit_bytes=58 * 1024 * 1024
        ),
        cost_estimate=pl.CostEstimate(
            flops=2 * count * TOK * weight_count,
            bytes_accessed=2 * weight_count,
            transcendentals=count * TOK * experts * hid,
        ),
    )(tokens, expert_ids, scores, gate_weight, up_weight, down_weight)


def choose(tokens, expert_ids, scores, gate_weight, up_weight, down_weight):
    groups, owners = lax.axis_size("grp"), lax.axis_size("ex")
    experts, width, hid = gate_weight.shape
    out_w = down_weight.shape[2]
    lanes = ceil_lanes(width + 256, 2 * PACK)
    fits = (
        tokens.shape[0] == TOK
        and lax.axis_size("side") == 2
        and groups == 4
        and owners == 4
        and hid % 128 == 0
        and out_w % 128 == 0
        and 256 <= out_w <= 2 * PACK * 128
        and width % 128 == 0
        and width - (2 * PACK - 1) * lanes > 0
        and experts * owners <= 128
        and experts * (2 * width * hid + groups * hid * out_w) * 2 <= 44 * 1024 * 1024
    )
    if not fits:
        return per_device(tokens, expert_ids, scores, gate_weight, up_weight, down_weight)
    dims = (groups, owners, experts, width, hid, out_w, lanes)
    return fused(dims, tokens, expert_ids, scores, gate_weight, up_weight, down_weight)


def solution(mesh):
    in_specs = (
        P(("grp", "ex"), "side"),
        P(("grp", "ex"), None),
        P(("grp", "ex"), None),
        P("ex", "side", "grp"),
        P("ex", "side", "grp"),
        P("ex", None, ("side", "grp")),
    )
    out_specs = P(("grp", "ex"), "side")
    return jax.shard_map(
        choose, mesh=mesh, in_specs=in_specs, out_specs=out_specs, check_vma=False
    )
```

time: 41.1 us -> 47.7 us (1.16)
  Pallas kernels: 39.4 us -> 46.1 us
    pallas_call x1, Pallas kernels: 39.4 us -> 46.1 us  [fused(): pl.pallas_call(functools.partial(fused_kernel, dims), out_shape=jax.Shape...]
where the time goes in v2:
time: 47.7 us; the launch traced here: 47.5 us
  Pallas kernels  46.1 us (97%)
  local copies, waits for them, and re-layouts  1.37 us (3%)
    pallas_call x1, Pallas kernels, fused(): pl.pallas_call(functools.partial(fused_kernel, dims), out_shape=jax.Shape...  46.1 us
    unnamed x1, local copies, waits for them, and re-layouts  1.37 us

profile of v2, /device:TPU:0, one launch (start us, length us, event | category | flops | bytes accessed | tf_op | source)
XLA Modules:
  0.0 47.5 jit_solution(3546466021451335786)
XLA Ops:
  0.0 46.1 %shard_map.64 = bf16[3,3584]{1,0:T(4,128)(2,1)} custom-call(bf16[3,3584]{1,0:T(4,128)(2,1)} %tok_hbm.1, s32[3,8]{1,0:T(4,128)} %ids_hbm.1, f32[3,8]{1,0:T(4,128)} %score_hbm.1, bf16[4,3584,512]{2,1,0:T(8,128)(2,1)} %gate_hbm.1, bf16[4,3584,512]{2,1,0:T(8,128)(2,1)} %up_hbm.1, bf16[4,2048,896]{2,1,0:T(8,128)(2,1)} %down_hbm.1), custom_call_target="tpu_custom_call" | custom-call | flops 2113929216 | bytes 44040192 | tf_op jit(solution)/shard_map/pallas_call | solution.py:444
  46.1 1.4 %copy.8 = bf16[3,3584]{1,0:T(4,128)(2,1)} copy(bf16[3,3584]{1,0:T(4,128)(2,1)} %shard_map.64) | data formatting | bytes 43008

commit v3 on v1

--- a/solution.py
+++ b/solution.py
@@ -105,13 +105,16 @@
 
 def fused_kernel(
     dims,
-    tok_ref,
-    ids_ref,
-    score_ref,
+    tok_hbm,
+    ids_hbm,
+    score_hbm,
     gate_hbm,
     up_hbm,
     down_hbm,
     out_ref,
+    tok_ref,
+    ids_ref,
+    score_ref,
     gate_v,
     up_v,
     down_v,
@@ -125,7 +128,9 @@
     acc,
     ret,
     back,
-    fin,
+    ret_grp,
+    back_grp,
+    in_sem,
     gate_sem,
     up_sem,
     down_sem,
@@ -137,6 +142,8 @@
     hid_recv,
     ret_send,
     ret_recv,
+    last_send,
+    last_recv,
 ):
     groups, owners, experts, width, hid, out_w, lanes, ret_lanes = dims
     count = groups * owners
@@ -155,23 +162,29 @@
             pltpu.make_async_copy(down_hbm.at[e], down_v.at[e], down_sem.at[e]),
         )
 
+    mesh_id = pl.DeviceIdType.MESH
+    along_ex = [{"ex": lax.rem(own + step, owners)} for step in range(1, owners)]
+    along_grp = [{"grp": lax.rem(grp + step, groups)} for step in range(1, groups)]
+    partners = along_ex + along_grp + [sibling]
+    inputs = [
+        pltpu.make_async_copy(source, target, in_sem.at[i])
+        for i, (source, target) in enumerate(
+            ((tok_hbm, tok_ref), (ids_hbm, ids_ref), (score_hbm, score_ref))
+        )
+    ]
+    for copy in inputs:
+        copy.start()
+    barrier = pltpu.get_barrier_semaphore()
+    for device in partners:
+        pl.semaphore_signal(barrier, inc=1, device_id=device, device_id_type=mesh_id)
     for e in range(experts):
         gate_copy, up_copy, _ = loads(e)
         gate_copy.start()
         up_copy.start()
     for e in range(experts):
         loads(e)[2].start()
-
-    def peer(step):
-        target = lax.rem(me + step, count)
-        return target, {"grp": target // owners, "ex": lax.rem(target, owners)}
-
-    barrier = pltpu.get_barrier_semaphore()
-    for step in range(1, count):
-        pl.semaphore_signal(
-            barrier, inc=1, device_id=peer(step)[1], device_id_type=pl.DeviceIdType.MESH
-        )
-    pl.semaphore_signal(barrier, inc=1, device_id=sibling, device_id_type=pl.DeviceIdType.MESH)
+    for copy in inputs:
+        copy.wait()
 
     lifted = jax.nn.sigmoid(score_ref[...])
     route = 2.5 * lifted / jnp.sum(lifted, axis=-1, keepdims=True)
@@ -197,22 +210,39 @@
     my_rows = pl.ds(pl.multiple_of(me * ROWS, ROWS), ROWS)
     gathered[my_rows, :] = packed
 
-    pl.semaphore_wait(barrier, count)
-
-    def token_copy(step):
-        return pltpu.make_async_remote_copy(
+    pl.semaphore_wait(barrier, len(partners))
+
+    line = pl.ds(pl.multiple_of(grp * owners * ROWS, owners * ROWS), owners * ROWS)
+    ex_copies = [
+        pltpu.make_async_remote_copy(
             src_ref=block,
             dst_ref=gathered.at[my_rows],
-            send_sem=tok_send.at[step - 1],
-            recv_sem=tok_recv.at[step - 1],
-            device_id=peer(step)[1],
-            device_id_type=pl.DeviceIdType.MESH,
-        )
-
-    token_copies = [token_copy(step) for step in range(1, count)]
-    for copy in token_copies:
+            send_sem=tok_send.at[i],
+            recv_sem=tok_recv.at[i],
+            device_id=device,
+            device_id_type=mesh_id,
+        )
+        for i, device in enumerate(along_ex)
+    ]
+    grp_copies = [
+        pltpu.make_async_remote_copy(
+            src_ref=gathered.at[line],
+            dst_ref=gathered.at[line],
+            send_sem=tok_send.at[owners - 1 + i],
+            recv_sem=tok_recv.at[owners - 1 + i],
+            device_id=device,
+            device_id_type=mesh_id,
+        )
+        for i, device in enumerate(along_grp)
+    ]
+    for copy in ex_copies:
         copy.start()
-    for copy in token_copies:
+    acc[...] = jnp.zeros_like(acc)
+    for copy in ex_copies:
+        copy.wait_recv()
+    for copy in grp_copies:
+        copy.start()
+    for copy in grp_copies:
         copy.wait_recv()
 
     weights = None
@@ -263,8 +293,6 @@
         hidden[e, grp] = (gate / (1.0 + jnp.exp(-gate)) * up).astype(jnp.bfloat16)
         for step in range(1, groups):
             hidden_copy(e, step).start()
-
-    acc[...] = jnp.zeros_like(acc)
 
     def down(e):
         loads(e)[2].wait()
@@ -293,31 +321,35 @@
     for e in range(1 if experts > 1 else 0, experts):
         down(e)
 
-    packed_out = jnp.zeros((rows, ret_lanes), jnp.float32)
-    for piece in range(acc.shape[1] // ret_lanes):
-        packed_out = packed_out + jnp.dot(
-            unpack_matrix(piece, tokens, rows, True),
-            acc[:, pl.ds(piece * ret_lanes, ret_lanes)].astype(jnp.bfloat16),
-            preferred_element_type=jnp.float32,
-        )
-    ret[...] = packed_out.astype(jnp.bfloat16)
-
-    def return_copy(step):
-        target, device = peer(step)
-        return pltpu.make_async_remote_copy(
-            src_ref=ret.at[pl.ds(pl.multiple_of(target * ROWS, ROWS), ROWS)],
-            dst_ref=back.at[my_rows],
-            send_sem=ret_send.at[step - 1],
-            recv_sem=ret_recv.at[step - 1],
+    line_rows = owners * ROWS
+    token = lax.broadcasted_iota(jnp.int32, (line_rows, tokens), 1)
+    row = lax.broadcasted_iota(jnp.int32, (line_rows, tokens), 0)
+    source = lax.shift_right_logical(token * 171, 9)
+    source_grp = sum((source >= owners * j).astype(jnp.int32) for j in range(1, groups))
+    target = (source - owners * source_grp) * ROWS + TOK * source_grp + (token - TOK * source)
+    by_owner = jnp.where(row == target, 1.0, 0.0).astype(jnp.bfloat16)
+    ret[...] = jnp.dot(
+        by_owner, acc[:, pl.ds(0, out_w)].astype(jnp.bfloat16), preferred_element_type=jnp.float32
+    ).astype(jnp.bfloat16)
+
+    def owner_rows(index):
+        return pl.ds(pl.multiple_of(index * ROWS, ROWS), ROWS)
+
+    return_copies = [
+        pltpu.make_async_remote_copy(
+            src_ref=ret.at[owner_rows(device["ex"])],
+            dst_ref=back.at[owner_rows(own)],
+            send_sem=ret_send.at[i],
+            recv_sem=ret_recv.at[i],
             device_id=device,
-            device_id_type=pl.DeviceIdType.MESH,
-        )
-
-    return_copies = [return_copy(step) for step in range(1, count)]
+            device_id_type=mesh_id,
+        )
+        for i, device in enumerate(along_ex)
+    ]
     for copy in return_copies:
         copy.start()
-    back[my_rows, :] = ret[my_rows, :]
-    for copy in token_copies:
+    back[owner_rows(own), :] = ret[owner_rows(own), :]
+    for copy in ex_copies + grp_copies:
         copy.wait_send()
     for e in range(experts):
         side_copy(e).wait_send()
@@ -325,18 +357,48 @@
             hidden_copy(e, step).wait_send()
     for copy in return_copies:
         copy.wait_recv()
+    total = back[pl.ds(0, ROWS), :].astype(jnp.float32)
+    for k in range(1, owners):
+        total = total + back[pl.ds(k * ROWS, ROWS), :].astype(jnp.float32)
+    total = total.astype(jnp.bfloat16)
+    if acc.shape[1] > out_w:
+        spread = jnp.zeros((ROWS, acc.shape[1] - out_w), jnp.bfloat16)
+        total = jnp.concatenate([total, spread], axis=1)
+    packed_out = jnp.zeros((groups * ROWS, ret_lanes), jnp.float32)
+    for piece in range(acc.shape[1] // ret_lanes):
+        packed_out = packed_out + jnp.dot(
+            unpack_matrix(piece, ROWS, groups * ROWS, True),
+            total[:, piece * ret_lanes : (piece + 1) * ret_lanes],
+            preferred_element_type=jnp.float32,
+        )
+    ret_grp[...] = packed_out.astype(jnp.bfloat16)
+    last_copies = [
+        pltpu.make_async_remote_copy(
+            src_ref=ret_grp.at[owner_rows(device["grp"])],
+            dst_ref=back_grp.at[owner_rows(grp)],
+            send_sem=last_send.at[i],
+            recv_sem=last_recv.at[i],
+            device_id=device,
+            device_id_type=mesh_id,
+        )
+        for i, device in enumerate(along_grp)
+    ]
+    for copy in last_copies:
+        copy.start()
+    back_grp[owner_rows(grp), :] = ret_grp[owner_rows(grp), :]
+    for copy in return_copies:
+        copy.wait_send()
+    for copy in last_copies:
+        copy.wait_recv()
     for j in range(groups):
-        total = back[pl.ds(j * owners * ROWS, ROWS), :].astype(jnp.float32)
-        for k in range(1, owners):
-            total = total + back[pl.ds((j * owners + k) * ROWS, ROWS), :].astype(jnp.float32)
-        fin[j] = total
+        final = back_grp[pl.ds(j * ROWS, ROWS), :].astype(jnp.float32)
         for piece in range(acc.shape[1] // ret_lanes):
             begin = piece * ret_lanes
             size = min(ret_lanes, out_w - begin)
-            out_ref[:, pl.ds(j * out_w + begin, size)] = fin[
-                j, pl.ds(TOK * piece, TOK), pl.ds(0, size)
+            out_ref[:, pl.ds(j * out_w + begin, size)] = final[
+                TOK * piece : TOK * (piece + 1), :size
             ].astype(jnp.bfloat16)
-    for copy in return_copies:
+    for copy in last_copies:
         copy.wait_send()
 
 
@@ -356,9 +418,12 @@
     return pl.pallas_call(
         functools.partial(fused_kernel, dims),
         out_shape=jax.ShapeDtypeStruct(tokens.shape, jnp.bfloat16),
-        in_specs=[vmem, vmem, vmem, hbm, hbm, hbm],
+        in_specs=[hbm] * 6,
         out_specs=vmem,
         scratch_shapes=[
+            pltpu.VMEM(tokens.shape, jnp.bfloat16),
+            pltpu.VMEM(expert_ids.shape, jnp.int32),
+            pltpu.VMEM(scores.shape, jnp.float32),
             pltpu.VMEM(gate_weight.shape, jnp.bfloat16),
             pltpu.VMEM(up_weight.shape, jnp.bfloat16),
             pltpu.VMEM(down_weight.shape, jnp.bfloat16),
@@ -370,20 +435,24 @@
             pltpu.VMEM((experts, count * TOK, 2 * hid), jnp.float32),
             pltpu.VMEM((experts, groups, count * TOK, hid), jnp.bfloat16),
             pltpu.VMEM((count * TOK, acc_w), jnp.float32),
-            pltpu.VMEM((rows, ret_lanes), jnp.bfloat16),
-            pltpu.VMEM((rows, ret_lanes), jnp.bfloat16),
-            pltpu.VMEM((groups, ROWS, ret_lanes), jnp.float32),
+            pltpu.VMEM((owners * ROWS, out_w), jnp.bfloat16),
+            pltpu.VMEM((owners * ROWS, out_w), jnp.bfloat16),
+            pltpu.VMEM((groups * ROWS, ret_lanes), jnp.bfloat16),
+            pltpu.VMEM((groups * ROWS, ret_lanes), jnp.bfloat16),
+            dma((3,)),
             dma((experts,)),
             dma((experts,)),
             dma((experts,)),
-            dma((count - 1,)),
-            dma((count - 1,)),
+            dma((owners + groups - 2,)),
+            dma((owners + groups - 2,)),
             dma((experts,)),
             dma((experts,)),
             dma((experts, groups - 1)),
             dma((experts, groups - 1)),
-            dma((count - 1,)),
-            dma((count - 1,)),
+            dma((owners - 1,)),
+            dma((owners - 1,)),
+            dma((groups - 1,)),
+            dma((groups - 1,)),
         ],
         compiler_params=pltpu.CompilerParams(
             collective_id=0, has_side_effects=True, vmem_limit_bytes=58 * 1024 * 1024
@@ -405,10 +474,11 @@
     fits = (
         tokens.shape[0] == TOK
         and lax.axis_size("side") == 2
-        and groups > 1
-        and groups * owners == 16
+        and groups == 4
+        and owners == 4
         and hid % 128 == 0
         and out_w % 128 == 0
+        and width % 128 == 0
         and width - (PACK - 1) * lanes > 0
         and experts * owners <= 128
         and experts * (2 * width * hid + groups * hid * out_w) * 2 <= 44 * 1024 * 1024

time: 41.1 us -> 39.7 us (0.966)
  Pallas kernels: 39.4 us -> 38.1 us
    pallas_call x1, Pallas kernels: 39.4 us -> 38.1 us  [fused(): pl.pallas_call(functools.partial(fused_kernel, dims), out_shape=jax.Shape...]
where the time goes in v3:
time: 39.7 us; the launch traced here: 39.5 us
  Pallas kernels  38.1 us (96%)
  local copies, waits for them, and re-layouts  1.37 us (3%)
    pallas_call x1, Pallas kernels, fused(): pl.pallas_call(functools.partial(fused_kernel, dims), out_shape=jax.Shape...  38.1 us
    unnamed x1, local copies, waits for them, and re-layouts  1.37 us

profile of v3, /device:TPU:0, one launch (start us, length us, event | category | flops | bytes accessed | tf_op | source)
XLA Modules:
  0.0 39.5 jit_solution(2686557754929622762)
XLA Ops:
  0.0 38.1 %shard_map.64 = bf16[3,3584]{1,0:T(4,128)(2,1)} custom-call(bf16[3,3584]{1,0:T(4,128)(2,1)} %tok_hbm.1, s32[3,8]{1,0:T(4,128)} %ids_hbm.1, f32[3,8]{1,0:T(4,128)} %score_hbm.1, bf16[4,3584,512]{2,1,0:T(8,128)(2,1)} %gate_hbm.1, bf16[4,3584,512]{2,1,0:T(8,128)(2,1)} %up_hbm.1, bf16[4,2048,896]{2,1,0:T(8,128)(2,1)} %down_hbm.1), custom_call_target="tpu_custom_call" | custom-call | flops 2113929216 | bytes 44040192 | tf_op jit(solution)/shard_map/pallas_call | solution.py:418
  38.1 1.4 %copy.8 = bf16[3,3584]{1,0:T(4,128)(2,1)} copy(bf16[3,3584]{1,0:T(4,128)(2,1)} %shard_map.64) | data formatting | bytes 43008
